TPU v7x, 256 devices: a whole 4x4x8 slice. The times are simulated.
256 devices in a mesh: gx: 4 (over y), gy: 8 (over z_lo, core), gz: 8 (over x, z_hi).
Axes of the slice: x: 4, y: 4, z: 8 (z_hi: 2, z_lo: 4; z = z_hi * 4 + z_lo), core: 2. Of those that a mesh axis runs over, the one named last changes fastest.
Arguments:
- residual_start: float32 [8, 16, 16, 81, 128], P('gx', 'gy', 'gz'), may hold values from -6 to 6
- patch_inverse: bfloat16 [8, 16, 16, 540, 540], P('gx', 'gy', 'gz'), may hold values from -0.05 to 0.4
- patch_order: int32 [8, 16, 16, 540], P('gx', 'gy', 'gz'), may hold values from 0 to 539, each once within a row
- element_matrix: float32 [8, 16, 16, 108, 108], P('gx', 'gy', 'gz'), may hold values from -1.6 to 6.5
- face_order: int32 [8, 16, 16, 6, 9], P('gx', 'gy', 'gz'), may hold values from 0 to 8, each once within a row
Outputs:
- solution: float32 [8, 16, 16, 81, 128], P('gx', 'gy', 'gz')
- residual: float32 [8, 16, 16, 81, 128], P('gx', 'gy', 'gz')
Inputs may be any that keep to these rules, and one draw needn't show every extreme that they name: `patch_order`: each row lists each of the 540 canonical rows of a star once. `face_order`: each face's row lists each of its 9 degrees of freedom once.
All inputs are finite; a program needn't handle non-finite values.
Results may differ from a plain program's by a relative error of at most 0.0068.
Values may be sent and summed in bfloat16 or wider, within the bound.
A program may use at most 128 MiB of HBM per device.

v0:
```python
import jax
import jax.numpy as jnp
from jax import lax
from jax.experimental import pallas as pl
from jax.experimental.pallas import tpu as pltpu
from jax.sharding import PartitionSpec as P

INNER = 54
FACE = 9
SWEEPS = 2
PATCH = 540
LOCAL = 108
STAR = 640
WIDE = 144
BLOCK = 96
MESH = pl.DeviceIdType.MESH
F32 = jnp.float32
BF16 = jnp.bfloat16

Z_HALO = 0
EARLY_X, EARLY_Y, EARLY_XY = 1, 2, 3
LATE_X, LATE_Y, LATE_XY = 4, 5, 6
BACK_X, BACK_Y, BACK_XY = 7, 8, 9
BACK2_X, BACK2_Y, BACK2_XY = 10, 11, 12
BACK_Z = 13
IMAGE_X, IMAGE_Y = 14, 16
IMAGE_Z = 18
COPIES = 19


def star_rows(order):
    one = lambda flag: flag.astype(jnp.int32)
    place = order
    for m in range(1, 8):
        place = place + 10 * one(order >= INNER * m)
    base = 8 * INNER
    place_x = order - 122
    place_y = order + 44
    place_z = order + 72
    for f in range(1, 4):
        place_x = place_x + 55 * one(order >= base + FACE * f)
        place_y = place_y + 7 * one(order >= base + FACE * (4 + f))
        place_z = place_z + 7 * one(order >= base + FACE * (8 + f))
    place = jnp.where(order >= base, place_x, place)
    place = jnp.where(order >= base + 4 * FACE, place_y, place)
    return jnp.where(order >= base + 8 * FACE, place_z, place)


def kernel(
    start_ref, inverse_ref, order_ref, matrix_ref, faces_ref,
    solution_ref, residual_ref,
    held, stars, high, low, rim, total, change, left,
    out_x, out_y, out_xy, in_x, in_y, in_xy, out_z, in_z,
    out_ix, out_iy, out_iz, in_ix, in_iy, in_iz,
    load_sem, send_sem, recv_sem,
):
    gx, gy, gz = lax.axis_index("gx"), lax.axis_index("gy"), lax.axis_index("gz")
    count_x, count_y, count_z = lax.axis_size("gx"), lax.axis_size("gy"), lax.axis_size("gz")
    up_x, down_x = lax.rem(gx + 1, count_x), lax.rem(gx + count_x - 1, count_x)
    first_y, last_y = gy == 0, gy == count_y - 1
    first_z, last_z = gz == 0, gz == count_z - 1
    not_first_y, not_last_y = gy > 0, gy < count_y - 1
    not_first_z, not_last_z = gz > 0, gz < count_z - 1

    load = pltpu.make_async_copy(inverse_ref, held, load_sem)
    load.start()

    def blank(i, carry):
        rim[i // 27, (i // 9) % 3, (i // 3) % 3, i % 3] = jnp.zeros((BLOCK, 128), BF16)
        return carry

    lax.fori_loop(0, SWEEPS * 27, blank, 0)

    barrier = pltpu.get_barrier_semaphore()

    def greet(device):
        pl.semaphore_signal(barrier, inc=1, device_id=device, device_id_type=MESH)

    greet((up_x, gy, gz))
    greet((down_x, gy, gz))

    @pl.when(not_last_y)
    def _():
        greet((gx, gy + 1, gz))
        greet((up_x, gy + 1, gz))

    @pl.when(not_first_y)
    def _():
        greet((gx, gy - 1, gz))
        greet((down_x, gy - 1, gz))

    @pl.when(not_last_z)
    def _():
        greet((gx, gy, gz + 1))

    @pl.when(not_first_z)
    def _():
        greet((gx, gy, gz - 1))

    always = None
    routes = {}

    def route(s, number, src, dst, device, sends, receives):
        copy = pltpu.make_async_remote_copy(
            src_ref=src, dst_ref=dst, send_sem=send_sem.at[s, number], recv_sem=recv_sem.at[s, number],
            device_id=device, device_id_type=MESH,
        )
        routes[s, number] = (copy, sends, receives)

    upper_y, lower_y = gy + 1, gy - 1
    for s in range(SWEEPS):
        here = rim.at[s]
        route(s, Z_HALO, here.at[1:3, 1:3, 2, 16:96], here.at[1:3, 1:3, 0, 16:96], (gx, gy, gz + 1),
              not_last_z, not_first_z)
        for x, y, xy, layers in ((EARLY_X, EARLY_Y, EARLY_XY, slice(1, 3)), (LATE_X, LATE_Y, LATE_XY, slice(0, 1))):
            route(s, x, here.at[2, 1:3, layers], here.at[0, 1:3, layers], (up_x, gy, gz), always, always)
            route(s, y, here.at[1:3, 2, layers], here.at[1:3, 0, layers], (gx, upper_y, gz), not_last_y, not_first_y)
            route(s, xy, here.at[2, 2, layers], here.at[0, 0, layers], (up_x, upper_y, gz), not_last_y, not_first_y)
        for x, y, xy, layers in ((BACK_X, BACK_Y, BACK_XY, slice(0, 1)), (BACK2_X, BACK2_Y, BACK2_XY, slice(1, 3))):
            route(s, x, out_x.at[s, layers], in_x.at[s, layers], (down_x, gy, gz), always, always)
            route(s, y, out_y.at[s, layers], in_y.at[s, layers], (gx, lower_y, gz), not_first_y, not_last_y)
            route(s, xy, out_xy.at[s, layers], in_xy.at[s, layers], (down_x, lower_y, gz), not_first_y, not_last_y)
        route(s, BACK_Z, out_z.at[s], in_z.at[s], (gx, gy, gz - 1), not_first_z, not_last_z)
        for l in (0, 1):
            route(s, IMAGE_X + l, out_ix.at[s, l], in_ix.at[s, l], (up_x, gy, gz), always, always)
            route(s, IMAGE_Y + l, out_iy.at[s, l], in_iy.at[s, l], (gx, upper_y, gz), not_last_y, not_first_y)
        route(s, IMAGE_Z, out_iz.at[s], in_iz.at[s], (gx, gy, gz + 1), not_last_z, not_first_z)

    def if_(flag, action):
        if flag is None:
            action()
        else:
            pl.when(flag)(action)

    def send(s, *numbers):
        for number in numbers:
            copy, sends, _ = routes[s, number]
            if_(sends, copy.start)

    def receive(s, number, use=None):
        copy, _, receives = routes[s, number]

        def action():
            copy.wait_recv()
            if use is not None:
                use()

        if_(receives, action)

    def clear_left():
        @pl.when(first_y)
        def _():
            left[:, 0, :, 80:96] = jnp.zeros((2, 3, 16, 128), F32)

        @pl.when(first_z)
        def _():
            left[:, :, 0, 0:16] = jnp.zeros((2, 2, 16, 128), F32)

    left[...] = jnp.zeros_like(left)
    for x in range(2):
        for y in range(2):
            for z in range(2):
                left[x, y, z + 1, 16:79] = start_ref[x, y, z, 0:63]
                left[x, y, z + 1, 80:89] = start_ref[x, y, z, 63:72]
                left[x, y, z, 0:9] = start_ref[x, y, z, 72:81]
    clear_left()

    def round_early(s):
        for x in range(2):
            for y in range(2):
                rim[s, x + 1, y + 1, 1] = left[x, y, 1].astype(BF16)
                rim[s, x + 1, y + 1, 2, 16:96] = left[x, y, 2, 16:96].astype(BF16)

    def round_late(s):
        for x in range(2):
            for y in range(2):
                rim[s, x + 1, y + 1, 0, 0:16] = left[x, y, 0, 0:16].astype(BF16)

    round_early(0)
    round_late(0)

    met = 2 + 2 * not_last_y.astype(jnp.int32) + 2 * not_first_y.astype(jnp.int32)
    met = met + not_last_z.astype(jnp.int32) + not_first_z.astype(jnp.int32)
    pl.semaphore_wait(barrier, met)

    send(0, Z_HALO, EARLY_X, EARLY_Y, EARLY_XY)

    def blank_sums(i, carry):
        s, x, y, l = i // 48, (i // 12) % 4, (i // 3) % 4, i % 3
        total[s, x, y, l] = jnp.zeros((BLOCK, 128), F32)
        change[s, x, y, l] = jnp.zeros((BLOCK, 128), F32)
        return carry

    lax.fori_loop(0, SWEEPS * 48, blank_sums, 0)

    dims_nt = (((1,), (1,)), ((), ()))

    lane = lax.broadcasted_iota(jnp.int32, (1, LOCAL), 1)
    face = sum((lane >= INNER + FACE * f).astype(jnp.int32) for f in range(1, 6))
    slot = lane - INNER - FACE * face
    spread = (lax.broadcasted_iota(jnp.int32, (FACE, LOCAL), 0) == slot).astype(F32)
    own_face = (lax.broadcasted_iota(jnp.int32, (6, LOCAL), 0) == face) & (lane >= INNER)
    base = jnp.where(lane < INNER, 16 + lane, 0)
    for f, offset in enumerate((70, 118, 80, 128, 96, 0)):
        base = base + jnp.where((lane >= INNER) & (face == f), offset, 0)
    base = base.astype(F32)
    wide_rows = lax.broadcasted_iota(jnp.int32, (WIDE, LOCAL), 0).astype(F32)

    def element(i, z):
        x, y = i // 2, i % 2
        listed = jnp.dot(faces_ref[x, y, z].astype(F32).astype(BF16), spread.astype(BF16), preferred_element_type=F32)
        place = base + jnp.sum(jnp.where(own_face, listed, 0.0), axis=0, keepdims=True)
        pick = jnp.where(wide_rows == place, 1.0, 0.0).astype(BF16)
        matrix = matrix_ref[x, y, z]
        upper = matrix.astype(BF16)
        lower = (matrix - upper.astype(F32)).astype(BF16)
        for part, ref in ((upper, high), (lower, low)):
            rows = jnp.dot(pick, part, preferred_element_type=F32).astype(BF16)
            ref[z, i] = lax.dot_general(rows, pick, dims_nt, preferred_element_type=F32).astype(BF16)

    def elements(i, carry):
        element(i, 0)
        element(i, 1)
        return carry

    lax.fori_loop(0, 4, elements, 0)

    star_iota = lax.broadcasted_iota(jnp.int32, (STAR, PATCH), 0)

    def prepare(c, first, last):
        def vertex(i, carry):
            x, y = i // 2, i % 2
            place = star_rows(order_ref[x, y, c : c + 1, :])
            pick = jnp.where(star_iota == place, 1.0, 0.0).astype(BF16)
            rows = jnp.dot(pick, held[x, y, c], preferred_element_type=F32).astype(BF16)
            stars[c, i] = lax.dot_general(rows, pick, dims_nt, preferred_element_type=F32).astype(BF16)
            return carry

        lax.fori_loop(first, last, vertex, 0)

    def solve(s, c):
        def vertex(i, carry):
            x, y = i // 2, i % 2
            pieces = []
            for p in (0, 1):
                for q in (0, 1):
                    for r in (0, 1):
                        pieces.append(rim[s, x + p, y + q, c + r, 16:80])
            for p in (0, 1):
                for r in (0, 1):
                    pieces.append(rim[s, x + p, y + 1, c + r, 80:96])
            for p in (0, 1):
                for q in (0, 1):
                    pieces.append(rim[s, x + p, y + q, c, 0:16])
            solved = jnp.dot(stars[c, i], jnp.concatenate(pieces, axis=0), preferred_element_type=F32)
            for p in (0, 1):
                for q in (0, 1):
                    for r in (0, 1):
                        m = 64 * (4 * p + 2 * q + r)
                        total[s, x + p, y + q, c + r, 16:80] += solved[m : m + 64]
            for p in (0, 1):
                for r in (0, 1):
                    m = 512 + 16 * (2 * p + r)
                    total[s, x + p, y + 1, c + r, 80:96] += solved[m : m + 16]
            for p in (0, 1):
                for q in (0, 1):
                    m = 576 + 16 * (2 * p + q)
                    total[s, x + p, y + q, c, 0:16] += solved[m : m + 16]
            return carry

        lax.fori_loop(0, 4, vertex, 0)

    def send_back(s, layers, numbers):
        for l in layers:
            for k in (1, 2):
                out_x[s, l, k - 1, 0:96] = total[s, 0, k, l].astype(BF16)
                out_x[s, l, k - 1, 96:112] = total[s, 1, k, l, 64:80].astype(BF16)
                out_y[s, l, k - 1, 0:96] = total[s, k, 0, l].astype(BF16)
                out_y[s, l, k - 1, 96:112] = total[s, k, 1, l, 80:96].astype(BF16)
            out_xy[s, l, 0:96] = total[s, 0, 0, l].astype(BF16)
            out_xy[s, l, 96:112] = total[s, 1, 0, l, 64:80].astype(BF16)
            out_xy[s, l, 112:128] = total[s, 0, 1, l, 80:96].astype(BF16)
        send(s, *numbers)

    def take_back(s, layers, numbers):
        def from_x():
            for l in layers:
                for k in (1, 2):
                    total[s, 2, k, l] += in_x[s, l, k - 1, 0:96].astype(F32)
                    total[s, 3, k, l, 64:80] += in_x[s, l, k - 1, 96:112].astype(F32)

        def from_y():
            for l in layers:
                for k in (1, 2):
                    total[s, k, 2, l] += in_y[s, l, k - 1, 0:96].astype(F32)
                    total[s, k, 3, l, 80:96] += in_y[s, l, k - 1, 96:112].astype(F32)

        def from_xy():
            for l in layers:
                total[s, 2, 2, l] += in_xy[s, l, 0:96].astype(F32)
                total[s, 3, 2, l, 64:80] += in_xy[s, l, 96:112].astype(F32)
                total[s, 2, 3, l, 80:96] += in_xy[s, l, 112:128].astype(F32)

        for number, use in zip(numbers, (from_x, from_y, from_xy)):
            receive(s, number, use)

    def send_back_z(s):
        for x in (1, 2):
            for y in (1, 2):
                m = BLOCK * (2 * x + y - 3)
                out_z[s, m : m + BLOCK] = total[s, x, y, 0].astype(BF16)
        for k in (1, 2):
            m = 384 + 16 * (k - 1)
            out_z[s, m : m + 16] = total[s, 3, k, 0, 64:80].astype(BF16)
            out_z[s, m + 32 : m + 48] = total[s, k, 3, 0, 80:96].astype(BF16)
        send(s, BACK_Z)

    def take_back_z(s):
        def use():
            for x in (1, 2):
                for y in (1, 2):
                    m = BLOCK * (2 * x + y - 3)
                    total[s, x, y, 2] += in_z[s, m : m + BLOCK].astype(F32)
            for k in (1, 2):
                m = 384 + 16 * (k - 1)
                total[s, 3, k, 2, 64:80] += in_z[s, m : m + 16].astype(F32)
                total[s, k, 3, 2, 80:96] += in_z[s, m + 32 : m + 48].astype(F32)

        receive(s, BACK_Z, use)

    def clear_total(s):
        @pl.when(first_y)
        def _():
            total[s, 1:3, 1, :, 80:96] = jnp.zeros((2, 3, 16, 128), F32)

        @pl.when(first_z)
        def _():
            total[s, 1:3, 1:3, 0, 0:16] = jnp.zeros((2, 2, 16, 128), F32)

    def images(s, l):
        def one(i, carry):
            x, y = i // 2 + 1, i % 2 + 1
            local = jnp.concatenate(
                [
                    total[s, x, y, l],
                    total[s, x, y, l - 1, 0:16],
                    total[s, x + 1, y, l, 64:80],
                    total[s, x, y + 1, l, 80:96],
                ],
                axis=0,
            )
            upper = local.astype(BF16)
            lower = (local - upper.astype(F32)).astype(BF16)
            image = jnp.dot(high[l - 1, i], upper, preferred_element_type=F32)
            image += jnp.dot(high[l - 1, i], lower, preferred_element_type=F32)
            image += jnp.dot(low[l - 1, i], upper, preferred_element_type=F32)
            change[s, x, y, l] += image[0:96]
            change[s, x, y, l - 1, 0:16] += image[96:112]
            change[s, x + 1, y, l, 64:80] += image[112:128]
            change[s, x, y + 1, l, 80:96] += image[128:144]
            return carry

        lax.fori_loop(0, 4, one, 0)

    def send_images(s, l):
        for k in (1, 2):
            m = 16 * (k - 1)
            out_ix[s, l - 1, m : m + 16] = change[s, 3, k, l, 64:80].astype(BF16)
            out_iy[s, l - 1, m : m + 16] = change[s, k, 3, l, 80:96].astype(BF16)
        send(s, IMAGE_X + l - 1, IMAGE_Y + l - 1)
        if l == 2:
            for x in (1, 2):
                for y in (1, 2):
                    m = 16 * (2 * x + y - 3)
                    out_iz[s, m : m + 16] = change[s, x, y, 2, 0:16].astype(BF16)
            send(s, IMAGE_Z)

    def take_images(s, l):
        def from_x():
            for k in (1, 2):
                m = 16 * (k - 1)
                change[s, 1, k, l, 64:80] += in_ix[s, l - 1, m : m + 16].astype(F32)

        def from_y():
            for k in (1, 2):
                m = 16 * (k - 1)
                change[s, k, 1, l, 80:96] += in_iy[s, l - 1, m : m + 16].astype(F32)

        receive(s, IMAGE_X + l - 1, from_x)
        receive(s, IMAGE_Y + l - 1, from_y)

    def take_images_z(s):
        def use():
            for x in (1, 2):
                for y in (1, 2):
                    m = 16 * (2 * x + y - 3)
                    change[s, x, y, 0, 0:16] += in_iz[s, m : m + 16].astype(F32)

        receive(s, IMAGE_Z, use)

    def update_early(s):
        for x in (1, 2):
            for y in (1, 2):
                left[x - 1, y - 1, 1] -= change[s, x, y, 1]
                left[x - 1, y - 1, 2, 16:96] -= change[s, x, y, 2, 16:96]
        clear_left()

    def update_late(s):
        for x in (1, 2):
            for y in (1, 2):
                left[x - 1, y - 1, 0, 0:16] -= change[s, x, y, 0, 0:16]
        clear_left()

    early = (EARLY_X, EARLY_Y, EARLY_XY)
    late = (LATE_X, LATE_Y, LATE_XY)
    back = (BACK_X, BACK_Y, BACK_XY)
    back2 = (BACK2_X, BACK2_Y, BACK2_XY)

    load.wait()
    prepare(0, 0, 4)
    for s in range(SWEEPS):
        if s > 0:
            for number in early:
                receive(s, number)
            solve(s, 1)
            take_images_z(s - 1)
            update_late(s - 1)
            round_late(s)
        receive(s, Z_HALO)
        send(s, *late)
        if s == 0:
            prepare(1, 0, 2)
            for number in early:
                receive(s, number)
        for number in late:
            receive(s, number)
        solve(s, 0)
        send_back(s, (0,), back)
        if s == 0:
            prepare(1, 2, 4)
        else:
            send_back(s, (1, 2), back2)
        take_back(s, (0,), back)
        send_back_z(s)
        if s == 0:
            solve(s, 1)
            send_back(s, (1, 2), back2)
        take_back(s, (1, 2), back2)
        clear_total(s)
        images(s, 1)
        send_images(s, 1)
        take_images(s, 1)
        take_back_z(s)
        clear_total(s)
        images(s, 2)
        send_images(s, 2)
        take_images(s, 2)
        update_early(s)
        if s < SWEEPS - 1:
            round_early(s + 1)
            send(s + 1, Z_HALO, *early)

    for x in range(2):
        for y in range(2):
            for z in range(2):
                block = total[0, x + 1, y + 1, z + 1] + total[1, x + 1, y + 1, z + 1]
                solution_ref[x, y, z, 0:63] = block[16:79]
                solution_ref[x, y, z, 63:72] = block[80:89]
                lower = total[0, x + 1, y + 1, z, 0:16] + total[1, x + 1, y + 1, z, 0:16]
                solution_ref[x, y, z, 72:81] = lower[0:9]
                residual_ref[x, y, z, 0:63] = left[x, y, z + 1, 16:79]
                residual_ref[x, y, z, 63:72] = left[x, y, z + 1, 80:89]
    take_images_z(SWEEPS - 1)
    update_late(SWEEPS - 1)
    for x in range(2):
        for y in range(2):
            for z in range(2):
                residual_ref[x, y, z, 72:81] = left[x, y, z, 0:9]

    for copy, sends, _ in routes.values():
        if_(sends, copy.wait_send)


def body(residual_start, patch_inverse, patch_order, element_matrix, face_order):
    shape = jax.ShapeDtypeStruct(residual_start.shape, F32)
    vmem = pl.BlockSpec(memory_space=pltpu.VMEM)
    return pl.pallas_call(
        kernel,
        out_shape=(shape, shape),
        in_specs=[vmem, pl.BlockSpec(memory_space=pl.ANY), vmem, vmem, vmem],
        out_specs=(vmem, vmem),
        scratch_shapes=[
            pltpu.VMEM((2, 2, 2, PATCH, PATCH), BF16),
            pltpu.VMEM((2, 4, STAR, STAR), BF16),
            pltpu.VMEM((2, 4, WIDE, WIDE), BF16),
            pltpu.VMEM((2, 4, WIDE, WIDE), BF16),
            pltpu.VMEM((SWEEPS, 3, 3, 3, BLOCK, 128), BF16),
            pltpu.VMEM((SWEEPS, 4, 4, 3, BLOCK, 128), F32),
            pltpu.VMEM((SWEEPS, 4, 4, 3, BLOCK, 128), F32),
            pltpu.VMEM((2, 2, 3, BLOCK, 128), F32),
            pltpu.VMEM((SWEEPS, 3, 2, 112, 128), BF16),
            pltpu.VMEM((SWEEPS, 3, 2, 112, 128), BF16),
            pltpu.VMEM((SWEEPS, 3, 128, 128), BF16),
            pltpu.VMEM((SWEEPS, 3, 2, 112, 128), BF16),
            pltpu.VMEM((SWEEPS, 3, 2, 112, 128), BF16),
            pltpu.VMEM((SWEEPS, 3, 128, 128), BF16),
            pltpu.VMEM((SWEEPS, 448, 128), BF16),
            pltpu.VMEM((SWEEPS, 448, 128), BF16),
            pltpu.VMEM((SWEEPS, 2, 32, 128), BF16),
            pltpu.VMEM((SWEEPS, 2, 32, 128), BF16),
            pltpu.VMEM((SWEEPS, 64, 128), BF16),
            pltpu.VMEM((SWEEPS, 2, 32, 128), BF16),
            pltpu.VMEM((SWEEPS, 2, 32, 128), BF16),
            pltpu.VMEM((SWEEPS, 64, 128), BF16),
            pltpu.SemaphoreType.DMA,
            pltpu.SemaphoreType.DMA((SWEEPS, COPIES)),
            pltpu.SemaphoreType.DMA((SWEEPS, COPIES)),
        ],
        compiler_params=pltpu.CompilerParams(
            collective_id=0, has_side_effects=True, vmem_limit_bytes=48 * 1024 * 1024
        ),
    )(residual_start, patch_inverse, patch_order, element_matrix, face_order)


def solution(mesh):
    return jax.shard_map(
        body,
        mesh=mesh,
        in_specs=(
            P("gx", "gy", "gz", None, None),
            P("gx", "gy", "gz", None, None),
            P("gx", "gy", "gz", None),
            P("gx", "gy", "gz", None, None),
            P("gx", "gy", "gz", None, None),
        ),
        out_specs=(P("gx", "gy", "gz", None, None), P("gx", "gy", "gz", None, None)),
        check_vma=False,
    )
```

profile of v0, /device:TPU:36, one launch (start us, length us, event | category | flops | bytes accessed | tf_op | source)
XLA Modules:
  0.0 90.1 jit_solution(6595327136014581527)
XLA Ops:
  0.6 0.7 copy.10.faces_ref
  1.4 1.0 %copy.7.start_ref = f32[2,2,2,81,128]{4,3,2,1,0:T(8,128)S(1)} copy(f32[2,2,2,81,128]{4,2,3,1,0:T(2,128)} %param.5) | data formatting | bytes 663552 | tf_op args[0]
  2.4 1.1 %copy.9.matrix_ref = f32[2,2,2,108,108]{4,3,2,1,0:T(8,128)S(1)} copy(f32[2,2,2,108,108]{4,2,3,1,0:T(2,128)} %param.8) | data formatting | bytes 746496 | tf_op args[3]
  3.4 0.0 copy-start
  3.4 5.7 %copy.8.inverse_ref = bf16[2,2,2,540,540]{4,3,2,1,0:T(8,128)(2,1)} copy(bf16[2,2,2,540,540]{4,2,3,1,0:T(2,128)(2,1)} %param.6) | data formatting | bytes 9331200 | tf_op args[1]
  9.1 0.0 copy-done
  9.1 79.1 %shard_map.68 = (f32[2,2,2,81,128]{4,3,2,1,0:T(8,128)S(1)}, f32[2,2,2,81,128]{4,3,2,1,0:T(8,128)S(1)}) custom-call(f32[2,2,2,81,128]{4,3,2,1,0:T(8,128)S(1)} %copy.7.start_ref, bf16[2,2,2,540,540]{4,3,2,1,0:T(8,128)(2,1)} %copy.8.inverse_ref, s32[2,2,2,540]{3,2,1,0:T(2,128)S(1)} %copy-done, f32[2,2,2,108,108]{4,3,2,1,0:T(8,128)S(1)} %copy.9.matrix_ref, ...), custom_call_target="tpu_custom_call" | custom-call | tf_op jit(solution)/shard_map/pallas_call | solution.py:487
  88.3 0.9 copy.11
  89.2 0.9 copy.12
Async XLA Ops:
  3.4 5.7 %copy-start = (s32[2,2,2,540]{3,2,1,0:T(2,128)S(1)}, s32[2,2,2,540]{3,2,1,0:T(2,128)}, u32[]{:S(2)}) copy-start(s32[2,2,2,540]{3,2,1,0:T(2,128)} %order_ref.1) | copy-start | bytes 51844
where the time goes:
time: 90.3 us; the launch traced here: 90.1 us
  Pallas kernels  79.1 us (88%)
  local copies, waits for them, and re-layouts  10.3 us (11%)
    pallas_call x1, Pallas kernels, body(): pl.pallas_call(kernel, out_shape=(shape, shape), in_specs=[vmem, pl.Block...  79.1 us
    unnamed x6, local copies, waits for them, and re-layouts  8.5 us

commit v1 on v0

--- a/solution.py
+++ b/solution.py
@@ -1,3 +1,5 @@
+import functools
+
 import jax
 import jax.numpy as jnp
 from jax import lax
@@ -25,31 +27,37 @@
 BACK_Z = 13
 IMAGE_X, IMAGE_Y = 14, 16
 IMAGE_Z = 18
-COPIES = 19
+Z_UPPER, Z_LOWER, Z_FACE, Z_LAST_X, Z_LAST_Y = 19, 20, 21, 22, 23
+BACK_Z_FIRST, BACK_Z_Y, BACK_Z_X = 24, 25, 26
+Z_FIRST, Z_SECOND = 27, 28
+COPIES = 29
+
+CELL_ROWS = [64 * (m // 2) + 352 * (m % 2) for m in range(8)]
+Y_ROWS = [256 + 16 * (g // 2) + (608 - 256) * (g % 2) for g in range(4)]
+Z_ROWS = [288 + 16 * h for h in range(4)]
+LOWER = 352
+SEGMENTS = (
+    [(INNER * m, CELL_ROWS[m]) for m in range(8)]
+    + [(8 * INNER + FACE * f, CELL_ROWS[4 + f] + INNER) for f in range(4)]
+    + [(8 * INNER + FACE * (4 + g), Y_ROWS[g]) for g in range(4)]
+    + [(8 * INNER + FACE * (8 + h), Z_ROWS[h]) for h in range(4)]
+)
 
 
 def star_rows(order):
-    one = lambda flag: flag.astype(jnp.int32)
-    place = order
-    for m in range(1, 8):
-        place = place + 10 * one(order >= INNER * m)
-    base = 8 * INNER
-    place_x = order - 122
-    place_y = order + 44
-    place_z = order + 72
-    for f in range(1, 4):
-        place_x = place_x + 55 * one(order >= base + FACE * f)
-        place_y = place_y + 7 * one(order >= base + FACE * (4 + f))
-        place_z = place_z + 7 * one(order >= base + FACE * (8 + f))
-    place = jnp.where(order >= base, place_x, place)
-    place = jnp.where(order >= base + 4 * FACE, place_y, place)
-    return jnp.where(order >= base + 8 * FACE, place_z, place)
+    place, shift = order, 0
+    for first, row in SEGMENTS:
+        step = row - first - shift
+        shift += step
+        if step:
+            place = place + step * (order >= first).astype(jnp.int32)
+    return place
 
 
 def kernel(
-    start_ref, inverse_ref, order_ref, matrix_ref, faces_ref,
+    start_any, inverse_any, order_any, matrix_any, faces_any,
     solution_ref, residual_ref,
-    held, stars, high, low, rim, total, change, left,
+    start_ref, order_ref, matrix_ref, faces_ref, pairs, wide, held, stars, high, low, rim, total, change, left,
     out_x, out_y, out_xy, in_x, in_y, in_xy, out_z, in_z,
     out_ix, out_iy, out_iz, in_ix, in_iy, in_iz,
     load_sem, send_sem, recv_sem,
@@ -62,15 +70,6 @@
     not_first_y, not_last_y = gy > 0, gy < count_y - 1
     not_first_z, not_last_z = gz > 0, gz < count_z - 1
 
-    load = pltpu.make_async_copy(inverse_ref, held, load_sem)
-    load.start()
-
-    def blank(i, carry):
-        rim[i // 27, (i // 9) % 3, (i // 3) % 3, i % 3] = jnp.zeros((BLOCK, 128), BF16)
-        return carry
-
-    lax.fori_loop(0, SWEEPS * 27, blank, 0)
-
     barrier = pltpu.get_barrier_semaphore()
 
     def greet(device):
@@ -96,6 +95,37 @@
     @pl.when(not_first_z)
     def _():
         greet((gx, gy, gz - 1))
+
+    inverses = inverse_any.reshape(2, 2, 2 * PATCH, PATCH)
+    loads = [pltpu.make_async_copy(start_any, start_ref, load_sem.at[0])]
+    for x in range(2):
+        for y in range(2):
+            loads.append(pltpu.make_async_copy(inverses.at[x, y], pairs.at[x, y], load_sem.at[1 + 2 * x + y]))
+    loads.append(pltpu.make_async_copy(order_any, order_ref, load_sem.at[5]))
+    loads.append(pltpu.make_async_copy(matrix_any, matrix_ref, load_sem.at[6]))
+    loads.append(pltpu.make_async_copy(faces_any, faces_ref, load_sem.at[7]))
+    for load in loads:
+        load.start()
+
+    def blank(x, y, layers, rows):
+        for s in range(SWEEPS):
+            for l in layers:
+                rim[s, x, y, l, rows] = jnp.zeros((rows.stop - rows.start, 128), BF16)
+
+    for x in (1, 2):
+        for y in (1, 2):
+            blank(x, y, (2,), slice(0, 16))
+
+    @pl.when(first_y)
+    def _():
+        for x in range(3):
+            blank(x, 0, (0, 1, 2), slice(0, 96))
+
+    @pl.when(first_z)
+    def _():
+        for x in (1, 2):
+            for y in (1, 2):
+                blank(x, y, (0,), slice(16, 96))
 
     always = None
     routes = {}
@@ -110,8 +140,22 @@
     upper_y, lower_y = gy + 1, gy - 1
     for s in range(SWEEPS):
         here = rim.at[s]
-        route(s, Z_HALO, here.at[1:3, 1:3, 2, 16:96], here.at[1:3, 1:3, 0, 16:96], (gx, gy, gz + 1),
-              not_last_z, not_first_z)
+        parts = (
+            (Z_FIRST, slice(2, 3), slice(1, 3), slice(16, 96)),
+            (Z_SECOND, slice(1, 2), slice(2, 3), slice(16, 96)),
+            (Z_HALO, slice(1, 2), slice(1, 2), slice(16, 96)),
+        )
+        if s > 0:
+            parts = (
+                (Z_UPPER, slice(2, 3), slice(1, 3), slice(16, 80)),
+                (Z_LOWER, slice(1, 2), slice(1, 3), slice(16, 64)),
+                (Z_FACE, slice(1, 3), slice(2, 3), slice(80, 96)),
+                (Z_LAST_X, slice(1, 2), slice(1, 3), slice(64, 80)),
+                (Z_LAST_Y, slice(1, 3), slice(1, 2), slice(80, 96)),
+            )
+        for number, x, y, rows in parts:
+            route(s, number, here.at[x, y, 2, rows], here.at[x, y, 0, rows], (gx, gy, gz + 1),
+                  not_last_z, not_first_z)
         for x, y, xy, layers in ((EARLY_X, EARLY_Y, EARLY_XY, slice(1, 3)), (LATE_X, LATE_Y, LATE_XY, slice(0, 1))):
             route(s, x, here.at[2, 1:3, layers], here.at[0, 1:3, layers], (up_x, gy, gz), always, always)
             route(s, y, here.at[1:3, 2, layers], here.at[1:3, 0, layers], (gx, upper_y, gz), not_last_y, not_first_y)
@@ -120,7 +164,13 @@
             route(s, x, out_x.at[s, layers], in_x.at[s, layers], (down_x, gy, gz), always, always)
             route(s, y, out_y.at[s, layers], in_y.at[s, layers], (gx, lower_y, gz), not_first_y, not_last_y)
             route(s, xy, out_xy.at[s, layers], in_xy.at[s, layers], (down_x, lower_y, gz), not_first_y, not_last_y)
-        route(s, BACK_Z, out_z.at[s], in_z.at[s], (gx, gy, gz - 1), not_first_z, not_last_z)
+        for number, rows in (
+            (BACK_Z_FIRST, slice(0, 96)),
+            (BACK_Z_Y, slice(96, 192)),
+            (BACK_Z_X, slice(192, 288)),
+            (BACK_Z, slice(288, 448)),
+        ):
+            route(s, number, out_z.at[s, rows], in_z.at[s, rows], (gx, gy, gz - 1), not_first_z, not_last_z)
         for l in (0, 1):
             route(s, IMAGE_X + l, out_ix.at[s, l], in_ix.at[s, l], (up_x, gy, gz), always, always)
             route(s, IMAGE_Y + l, out_iy.at[s, l], in_iy.at[s, l], (gx, upper_y, gz), not_last_y, not_first_y)
@@ -157,12 +207,13 @@
             left[:, :, 0, 0:16] = jnp.zeros((2, 2, 16, 128), F32)
 
     left[...] = jnp.zeros_like(left)
+    loads[0].wait()
     for x in range(2):
         for y in range(2):
             for z in range(2):
-                left[x, y, z + 1, 16:79] = start_ref[x, y, z, 0:63]
-                left[x, y, z + 1, 80:89] = start_ref[x, y, z, 63:72]
-                left[x, y, z, 0:9] = start_ref[x, y, z, 72:81]
+                left[x, y, z + 1, 16:79] = start_ref[x, y, 0:63, z, :]
+                left[x, y, z + 1, 80:89] = start_ref[x, y, 63:72, z, :]
+                left[x, y, z, 0:9] = start_ref[x, y, 72:81, z, :]
     clear_left()
 
     def round_early(s):
@@ -176,6 +227,12 @@
             for y in range(2):
                 rim[s, x + 1, y + 1, 0, 0:16] = left[x, y, 0, 0:16].astype(BF16)
 
+    def round_faces(s):
+        for l in (1, 2):
+            for k in range(2):
+                rim[s, 1, k + 1, l, 64:80] = left[0, k, l, 64:80].astype(BF16)
+                rim[s, k + 1, 1, l, 80:96] = left[k, 0, l, 80:96].astype(BF16)
+
     round_early(0)
     round_late(0)
 
@@ -183,15 +240,21 @@
     met = met + not_last_z.astype(jnp.int32) + not_first_z.astype(jnp.int32)
     pl.semaphore_wait(barrier, met)
 
-    send(0, Z_HALO, EARLY_X, EARLY_Y, EARLY_XY)
-
-    def blank_sums(i, carry):
-        s, x, y, l = i // 48, (i // 12) % 4, (i // 3) % 4, i % 3
-        total[s, x, y, l] = jnp.zeros((BLOCK, 128), F32)
-        change[s, x, y, l] = jnp.zeros((BLOCK, 128), F32)
-        return carry
-
-    lax.fori_loop(0, SWEEPS * 48, blank_sums, 0)
+    send(0, Z_FIRST, Z_SECOND, Z_HALO)
+
+    def blank_total(s):
+        def one(i, carry):
+            total[s, i // 12, (i // 3) % 4, i % 3] = jnp.zeros((BLOCK, 128), F32)
+            return carry
+
+        lax.fori_loop(0, 48, one, 0)
+
+    def blank_change():
+        def one(i, carry):
+            change[i // 48, (i // 12) % 4, (i // 3) % 4, i % 3] = jnp.zeros((BLOCK, 128), F32)
+            return carry
+
+        lax.fori_loop(0, SWEEPS * 48, one, 0)
 
     dims_nt = (((1,), (1,)), ((), ()))
 
@@ -208,10 +271,10 @@
 
     def element(i, z):
         x, y = i // 2, i % 2
-        listed = jnp.dot(faces_ref[x, y, z].astype(F32).astype(BF16), spread.astype(BF16), preferred_element_type=F32)
+        listed = jnp.dot(faces_ref[x, y, :, z, :].astype(F32).astype(BF16), spread.astype(BF16), preferred_element_type=F32)
         place = base + jnp.sum(jnp.where(own_face, listed, 0.0), axis=0, keepdims=True)
         pick = jnp.where(wide_rows == place, 1.0, 0.0).astype(BF16)
-        matrix = matrix_ref[x, y, z]
+        matrix = matrix_ref[x, y, :, z, :]
         upper = matrix.astype(BF16)
         lower = (matrix - upper.astype(F32)).astype(BF16)
         for part, ref in ((upper, high), (lower, low)):
@@ -223,7 +286,6 @@
         element(i, 1)
         return carry
 
-    lax.fori_loop(0, 4, elements, 0)
 
     star_iota = lax.broadcasted_iota(jnp.int32, (STAR, PATCH), 0)
 
@@ -238,37 +300,41 @@
 
         lax.fori_loop(first, last, vertex, 0)
 
-    def solve(s, c):
-        def vertex(i, carry):
-            x, y = i // 2, i % 2
-            pieces = []
-            for p in (0, 1):
-                for q in (0, 1):
-                    for r in (0, 1):
-                        pieces.append(rim[s, x + p, y + q, c + r, 16:80])
-            for p in (0, 1):
-                for r in (0, 1):
-                    pieces.append(rim[s, x + p, y + 1, c + r, 80:96])
-            for p in (0, 1):
-                for q in (0, 1):
-                    pieces.append(rim[s, x + p, y + q, c, 0:16])
-            solved = jnp.dot(stars[c, i], jnp.concatenate(pieces, axis=0), preferred_element_type=F32)
-            for p in (0, 1):
-                for q in (0, 1):
-                    for r in (0, 1):
-                        m = 64 * (4 * p + 2 * q + r)
-                        total[s, x + p, y + q, c + r, 16:80] += solved[m : m + 64]
-            for p in (0, 1):
-                for r in (0, 1):
-                    m = 512 + 16 * (2 * p + r)
-                    total[s, x + p, y + 1, c + r, 80:96] += solved[m : m + 16]
-            for p in (0, 1):
-                for q in (0, 1):
-                    m = 576 + 16 * (2 * p + q)
-                    total[s, x + p, y + q, c, 0:16] += solved[m : m + 16]
-            return carry
-
-        lax.fori_loop(0, 4, vertex, 0)
+    def star(s, c, x, y):
+        pieces = []
+        for p in (0, 1):
+            for q in (0, 1):
+                pieces.append(rim[s, x + p, y + q, c, 16:80])
+        for p in (0, 1):
+            pieces.append(rim[s, x + p, y + 1, c, 80:96])
+        for p in (0, 1):
+            for q in (0, 1):
+                pieces.append(rim[s, x + p, y + q, c, 0:16])
+        for p in (0, 1):
+            for q in (0, 1):
+                pieces.append(rim[s, x + p, y + q, c + 1, 16:80])
+        for p in (0, 1):
+            pieces.append(rim[s, x + p, y + 1, c + 1, 80:96])
+        return jnp.concatenate(pieces, axis=0)
+
+    def solve(s, c, upper):
+        first, last = (LOWER, STAR) if upper else (0, LOWER)
+        solved = {}
+        for x in (0, 1):
+            for y in (0, 1):
+                solved[x, y] = jnp.dot(stars[c, 2 * x + y, first:last], star(s, c, x, y), preferred_element_type=F32)
+        l = c + 1 if upper else c
+        for x in range(3):
+            for y in range(3):
+                near = [(x - p, y - q, p, q) for p in (0, 1) for q in (0, 1) if 0 <= x - p < 2 and 0 <= y - q < 2]
+                cell = [solved[i, j][64 * (2 * p + q) : 64 * (2 * p + q) + 64] for i, j, p, q in near]
+                total[s, x, y, l, 16:80] += functools.reduce(jnp.add, cell)
+                side = [solved[i, j][256 + 16 * p : 272 + 16 * p] for i, j, p, q in near if q == 1]
+                if side:
+                    total[s, x, y, l, 80:96] += functools.reduce(jnp.add, side)
+                if not upper:
+                    base = [solved[i, j][288 + 16 * (2 * p + q) : 304 + 16 * (2 * p + q)] for i, j, p, q in near]
+                    total[s, x, y, l, 0:16] += functools.reduce(jnp.add, base)
 
     def send_back(s, layers, numbers):
         for l in layers:
@@ -301,14 +367,20 @@
                 total[s, 3, 2, l, 64:80] += in_xy[s, l, 96:112].astype(F32)
                 total[s, 2, 3, l, 80:96] += in_xy[s, l, 112:128].astype(F32)
 
-        for number, use in zip(numbers, (from_x, from_y, from_xy)):
+        for number, use, then in ((numbers[1], from_y, BACK_Z_Y), (numbers[0], from_x, BACK_Z_X), (numbers[2], from_xy, None)):
             receive(s, number, use)
-
-    def send_back_z(s):
-        for x in (1, 2):
-            for y in (1, 2):
+            if then is not None and layers == (0,):
+                x, y = (1, 2) if then == BACK_Z_Y else (2, 1)
                 m = BLOCK * (2 * x + y - 3)
                 out_z[s, m : m + BLOCK] = total[s, x, y, 0].astype(BF16)
+                send(s, then)
+
+    def send_back_z_first(s):
+        out_z[s, 0:BLOCK] = total[s, 1, 1, 0].astype(BF16)
+        send(s, BACK_Z_FIRST)
+
+    def send_back_z(s):
+        out_z[s, 3 * BLOCK : 4 * BLOCK] = total[s, 2, 2, 0].astype(BF16)
         for k in (1, 2):
             m = 384 + 16 * (k - 1)
             out_z[s, m : m + 16] = total[s, 3, k, 0, 64:80].astype(BF16)
@@ -326,6 +398,9 @@
                 total[s, 3, k, 2, 64:80] += in_z[s, m : m + 16].astype(F32)
                 total[s, k, 3, 2, 80:96] += in_z[s, m + 32 : m + 48].astype(F32)
 
+        receive(s, BACK_Z_FIRST)
+        receive(s, BACK_Z_Y)
+        receive(s, BACK_Z_X)
         receive(s, BACK_Z, use)
 
     def clear_total(s):
@@ -338,53 +413,49 @@
             total[s, 1:3, 1:3, 0, 0:16] = jnp.zeros((2, 2, 16, 128), F32)
 
     def images(s, l):
-        def one(i, carry):
-            x, y = i // 2 + 1, i % 2 + 1
-            local = jnp.concatenate(
-                [
-                    total[s, x, y, l],
-                    total[s, x, y, l - 1, 0:16],
-                    total[s, x + 1, y, l, 64:80],
-                    total[s, x, y + 1, l, 80:96],
-                ],
-                axis=0,
-            )
-            upper = local.astype(BF16)
-            lower = (local - upper.astype(F32)).astype(BF16)
-            image = jnp.dot(high[l - 1, i], upper, preferred_element_type=F32)
-            image += jnp.dot(high[l - 1, i], lower, preferred_element_type=F32)
-            image += jnp.dot(low[l - 1, i], upper, preferred_element_type=F32)
-            change[s, x, y, l] += image[0:96]
-            change[s, x, y, l - 1, 0:16] += image[96:112]
-            change[s, x + 1, y, l, 64:80] += image[112:128]
-            change[s, x, y + 1, l, 80:96] += image[128:144]
-            return carry
-
-        lax.fori_loop(0, 4, one, 0)
+        for x in (1, 2):
+            for y in (1, 2):
+                i = 2 * x + y - 3
+                local = jnp.concatenate(
+                    [
+                        total[s, x, y, l],
+                        total[s, x, y, l - 1, 0:16],
+                        total[s, x + 1, y, l, 64:80],
+                        total[s, x, y + 1, l, 80:96],
+                    ],
+                    axis=0,
+                )
+                upper = local.astype(BF16)
+                lower = (local - upper.astype(F32)).astype(BF16)
+                image = jnp.dot(high[l - 1, i], upper, preferred_element_type=F32)
+                image += jnp.dot(high[l - 1, i], lower, preferred_element_type=F32)
+                image += jnp.dot(low[l - 1, i], upper, preferred_element_type=F32)
+                change[s, x, y, l] += image[0:96]
+                change[s, x, y, l - 1, 0:16] += image[96:112]
+                change[s, x + 1, y, l, 64:80] += image[112:128]
+                change[s, x, y + 1, l, 80:96] += image[128:144]
 
     def send_images(s, l):
-        for k in (1, 2):
-            m = 16 * (k - 1)
-            out_ix[s, l - 1, m : m + 16] = change[s, 3, k, l, 64:80].astype(BF16)
-            out_iy[s, l - 1, m : m + 16] = change[s, k, 3, l, 80:96].astype(BF16)
-        send(s, IMAGE_X + l - 1, IMAGE_Y + l - 1)
         if l == 2:
             for x in (1, 2):
                 for y in (1, 2):
                     m = 16 * (2 * x + y - 3)
                     out_iz[s, m : m + 16] = change[s, x, y, 2, 0:16].astype(BF16)
             send(s, IMAGE_Z)
+        for k in (1, 2):
+            m = 16 * (k - 1)
+            out_ix[s, l - 1, m : m + 16] = change[s, 3, k, l, 64:80].astype(BF16)
+            out_iy[s, l - 1, m : m + 16] = change[s, k, 3, l, 80:96].astype(BF16)
+        send(s, IMAGE_X + l - 1, IMAGE_Y + l - 1)
 
     def take_images(s, l):
         def from_x():
-            for k in (1, 2):
-                m = 16 * (k - 1)
-                change[s, 1, k, l, 64:80] += in_ix[s, l - 1, m : m + 16].astype(F32)
+            for k in (0, 1):
+                left[0, k, l, 64:80] -= in_ix[s, l - 1, 16 * k : 16 * k + 16].astype(F32)
 
         def from_y():
-            for k in (1, 2):
-                m = 16 * (k - 1)
-                change[s, k, 1, l, 80:96] += in_iy[s, l - 1, m : m + 16].astype(F32)
+            for k in (0, 1):
+                left[k, 0, l, 80:96] -= in_iy[s, l - 1, 16 * k : 16 * k + 16].astype(F32)
 
         receive(s, IMAGE_X + l - 1, from_x)
         receive(s, IMAGE_Y + l - 1, from_y)
@@ -415,81 +486,128 @@
     late = (LATE_X, LATE_Y, LATE_XY)
     back = (BACK_X, BACK_Y, BACK_XY)
     back2 = (BACK2_X, BACK2_Y, BACK2_XY)
-
-    load.wait()
-    prepare(0, 0, 4)
+    z_early = (Z_UPPER, Z_LOWER, Z_FACE)
+    z_late = (Z_LAST_X, Z_LAST_Y)
+
+    blank_total(0)
+    for load in loads[1:]:
+        load.wait()
+
+    def separate(i, carry):
+        x, y = i // 2, i % 2
+        for k in range(5):
+            width = min(128, PATCH - 128 * k)
+            wide[k, :, 0:width] = pairs[x, y, :, 128 * k : 128 * k + width].astype(F32)
+        for z in range(2):
+            for k in range(5):
+                width = min(128, PATCH - 128 * k)
+                rows = wide[k, pl.ds(z, PATCH, stride=2), :].astype(BF16)
+                held[x, y, z, :, 128 * k : 128 * k + width] = rows[:, 0:width]
+        return carry
+
+    lax.fori_loop(0, 4, separate, 0)
+    send(0, *early)
+    prepare(0, 0, 3)
     for s in range(SWEEPS):
-        if s > 0:
+        if s == 0:
+            receive(s, Z_FIRST)
+            send(s, LATE_X, LATE_XY)
+            receive(s, Z_SECOND)
+            send(s, LATE_Y)
+            prepare(0, 3, 4)
+            receive(s, Z_HALO)
+            prepare(1, 0, 1)
             for number in early:
                 receive(s, number)
-            solve(s, 1)
+        else:
+            for number in early:
+                receive(s, number)
+            solve(s, 1, False)
+            solve(s, 1, True)
             take_images_z(s - 1)
             update_late(s - 1)
             round_late(s)
-        receive(s, Z_HALO)
-        send(s, *late)
-        if s == 0:
-            prepare(1, 0, 2)
-            for number in early:
+            for number in z_early + z_late:
                 receive(s, number)
+            send(s, *late)
         for number in late:
             receive(s, number)
-        solve(s, 0)
+        solve(s, 0, False)
+        send_back_z_first(s)
         send_back(s, (0,), back)
+        solve(s, 0, True)
         if s == 0:
-            prepare(1, 2, 4)
+            prepare(1, 1, 3)
         else:
             send_back(s, (1, 2), back2)
         take_back(s, (0,), back)
         send_back_z(s)
         if s == 0:
-            solve(s, 1)
+            prepare(1, 3, 4)
+            solve(s, 1, False)
+            solve(s, 1, True)
             send_back(s, (1, 2), back2)
+            lax.fori_loop(0, 4, elements, 0)
+            blank_change()
+            blank_total(1)
         take_back(s, (1, 2), back2)
         clear_total(s)
         images(s, 1)
         send_images(s, 1)
-        take_images(s, 1)
         take_back_z(s)
         clear_total(s)
         images(s, 2)
         send_images(s, 2)
-        take_images(s, 2)
         update_early(s)
         if s < SWEEPS - 1:
             round_early(s + 1)
-            send(s + 1, Z_HALO, *early)
+            send(s + 1, *z_early)
+        take_images(s, 1)
+        take_images(s, 2)
+        clear_left()
+        if s < SWEEPS - 1:
+            round_faces(s + 1)
+            send(s + 1, *z_late)
+            send(s + 1, *early)
 
     for x in range(2):
         for y in range(2):
             for z in range(2):
                 block = total[0, x + 1, y + 1, z + 1] + total[1, x + 1, y + 1, z + 1]
-                solution_ref[x, y, z, 0:63] = block[16:79]
-                solution_ref[x, y, z, 63:72] = block[80:89]
+                solution_ref[x, y, 0:63, z, :] = block[16:79]
+                solution_ref[x, y, 63:72, z, :] = block[80:89]
                 lower = total[0, x + 1, y + 1, z, 0:16] + total[1, x + 1, y + 1, z, 0:16]
-                solution_ref[x, y, z, 72:81] = lower[0:9]
-                residual_ref[x, y, z, 0:63] = left[x, y, z + 1, 16:79]
-                residual_ref[x, y, z, 63:72] = left[x, y, z + 1, 80:89]
+                solution_ref[x, y, 72:81, z, :] = lower[0:9]
+                residual_ref[x, y, 0:63, z, :] = left[x, y, z + 1, 16:79]
+                residual_ref[x, y, 63:72, z, :] = left[x, y, z + 1, 80:89]
     take_images_z(SWEEPS - 1)
     update_late(SWEEPS - 1)
     for x in range(2):
         for y in range(2):
             for z in range(2):
-                residual_ref[x, y, z, 72:81] = left[x, y, z, 0:9]
+                residual_ref[x, y, 72:81, z, :] = left[x, y, z, 0:9]
 
     for copy, sends, _ in routes.values():
         if_(sends, copy.wait_send)
 
 
 def body(residual_start, patch_inverse, patch_order, element_matrix, face_order):
+    swapped = lambda value: jnp.transpose(value, (0, 1, 3, 2, 4))
+    residual_start = swapped(residual_start)
     shape = jax.ShapeDtypeStruct(residual_start.shape, F32)
     vmem = pl.BlockSpec(memory_space=pltpu.VMEM)
-    return pl.pallas_call(
+    total, left = pl.pallas_call(
         kernel,
         out_shape=(shape, shape),
-        in_specs=[vmem, pl.BlockSpec(memory_space=pl.ANY), vmem, vmem, vmem],
+        in_specs=[pl.BlockSpec(memory_space=pltpu.HBM)] * 5,
         out_specs=(vmem, vmem),
         scratch_shapes=[
+            pltpu.VMEM(residual_start.shape, F32),
+            pltpu.VMEM(patch_order.shape, jnp.int32),
+            pltpu.VMEM((2, 2, LOCAL, 2, LOCAL), F32),
+            pltpu.VMEM((2, 2, 6, 2, FACE), jnp.int32),
+            pltpu.VMEM((2, 2, 2 * PATCH, PATCH), BF16),
+            pltpu.VMEM((5, 2 * PATCH, 128), F32),
             pltpu.VMEM((2, 2, 2, PATCH, PATCH), BF16),
             pltpu.VMEM((2, 4, STAR, STAR), BF16),
             pltpu.VMEM((2, 4, WIDE, WIDE), BF16),
@@ -512,14 +630,33 @@
             pltpu.VMEM((SWEEPS, 2, 32, 128), BF16),
             pltpu.VMEM((SWEEPS, 2, 32, 128), BF16),
             pltpu.VMEM((SWEEPS, 64, 128), BF16),
-            pltpu.SemaphoreType.DMA,
+            pltpu.SemaphoreType.DMA((8,)),
             pltpu.SemaphoreType.DMA((SWEEPS, COPIES)),
             pltpu.SemaphoreType.DMA((SWEEPS, COPIES)),
         ],
         compiler_params=pltpu.CompilerParams(
-            collective_id=0, has_side_effects=True, vmem_limit_bytes=48 * 1024 * 1024
+            collective_id=0, has_side_effects=True, vmem_limit_bytes=60 * 1024 * 1024
         ),
-    )(residual_start, patch_inverse, patch_order, element_matrix, face_order)
+    )(residual_start, swapped(patch_inverse), patch_order, swapped(element_matrix), swapped(face_order))
+
+    def finish(first, second, first_out, second_out, sem):
+        copies = [
+            pltpu.make_async_copy(first, first_out, sem.at[0]),
+            pltpu.make_async_copy(second, second_out, sem.at[1]),
+        ]
+        for copy in copies:
+            copy.start()
+        for copy in copies:
+            copy.wait()
+
+    total, left = pl.pallas_call(
+        finish,
+        out_shape=(shape, shape),
+        in_specs=[vmem, vmem],
+        out_specs=(pl.BlockSpec(memory_space=pltpu.HBM), pl.BlockSpec(memory_space=pltpu.HBM)),
+        scratch_shapes=[pltpu.SemaphoreType.DMA((2,))],
+    )(total, left)
+    return swapped(total), swapped(left)
 
 
 def solution(mesh):

time: 90.3 us -> 71.5 us (0.79)
  local copies, waits for them, and re-layouts: 10.3 us -> 0 us
  Pallas kernels: 79.1 us -> 70.6 us
    pallas_call x1 -> x2, Pallas kernels: 79.1 us -> 70.6 us  [the longest x1 68.6 us: body(): pl.pallas_call(kernel, out_shape=(shape, shape), in_specs=[pl.BlockSpec(m...]
    unnamed x6 -> x0, local copies, waits for them, and re-layouts: 8.5 us -> none
    pallas_call x2 -> x0, local copies, waits for them, and re-layouts: 1.79 us -> none  [body(): pl.pallas_call(kernel, out_shape=(shape, shape), in_specs=[vmem, pl.Block...]
where the time goes in v1:
time: 71.5 us; the launch traced here: 71.4 us
  Pallas kernels  70.6 us (99%)
  between operations  0.8 us (1%)
    pallas_call x1, Pallas kernels, body(): pl.pallas_call(kernel, out_shape=(shape, shape), in_specs=[pl.BlockSpec(m...  68.6 us
    pallas_call x1, Pallas kernels, body(): pl.pallas_call(finish, out_shape=(shape, shape), in_specs=[vmem, vmem], o...  1.93 us

profile of v1, /device:TPU:36, one launch (start us, length us, event | category | flops | bytes accessed | tf_op | source)
XLA Modules:
  0.0 71.4 jit_solution(9218915949061942695)
XLA Ops:
  0.6 68.6 %shard_map.68 = (f32[2,2,81,2,128]{4,3,2,1,0:T(2,128)}, f32[2,2,81,2,128]{4,3,2,1,0:T(2,128)}) custom-call(f32[2,2,81,2,128]{4,3,2,1,0:T(2,128)} %bitcast.8, bf16[2,2,540,2,540]{4,3,2,1,0:T(2,128)(2,1)} %bitcast.6, s32[2,2,2,540]{3,2,1,0:T(2,128)} %order_any.1, f32[2,2,108,2,108]{4,3,2,1,0:T(2,128)} %bitcast.7, s32[2,2,6,2,9]{4,3,2,1,0:T(2,128)} %bitcast.9), custom_call_target="tpu_custom_call" | custom-call | tf_op jit(solution)/shard_map/pallas_call | solution.py:599
  69.3 1.9 %shard_map.69 = (f32[2,2,81,2,128]{4,3,2,1,0:T(2,128)}, f32[2,2,81,2,128]{4,3,2,1,0:T(2,128)}) custom-call(f32[2,2,81,2,128]{4,3,2,1,0:T(2,128)} %get-tuple-element.6.first, f32[2,2,81,2,128]{4,3,2,1,0:T(2,128)} %get-tuple-element.7.second), custom_call_target="tpu_custom_call" | custom-call | tf_op jit(solution)/shard_map/pallas_call | solution.py:652

commit v2 on v1

--- a/solution.py
+++ b/solution.py
@@ -249,12 +249,12 @@
 
         lax.fori_loop(0, 48, one, 0)
 
-    def blank_change():
+    def blank_change(s):
         def one(i, carry):
-            change[i // 48, (i // 12) % 4, (i // 3) % 4, i % 3] = jnp.zeros((BLOCK, 128), F32)
+            change[s, i // 12, (i // 3) % 4, i % 3] = jnp.zeros((BLOCK, 128), F32)
             return carry
 
-        lax.fori_loop(0, SWEEPS * 48, one, 0)
+        lax.fori_loop(0, 48, one, 0)
 
     dims_nt = (((1,), (1,)), ((), ()))
 
@@ -482,6 +482,19 @@
                 left[x - 1, y - 1, 0, 0:16] -= change[s, x, y, 0, 0:16]
         clear_left()
 
+    def write_early():
+        for x in range(2):
+            for y in range(2):
+                for z in range(2):
+                    block = total[0, x + 1, y + 1, z + 1] + total[1, x + 1, y + 1, z + 1]
+                    solution_ref[x, y, 0:63, z, :] = block[16:79]
+                    solution_ref[x, y, 63:72, z, :] = block[80:89]
+                    lower = total[0, x + 1, y + 1, z, 0:16] + total[1, x + 1, y + 1, z, 0:16]
+                    solution_ref[x, y, 72:81, z, :] = lower[0:9]
+                    residual_ref[x, y, 0:63, z, :] = left[x, y, z + 1, 16:79]
+                    residual_ref[x, y, 63:72, z, :] = left[x, y, z + 1, 80:89]
+                residual_ref[x, y, 72:81, 1, :] = left[x, y, 1, 0:9]
+
     early = (EARLY_X, EARLY_Y, EARLY_XY)
     late = (LATE_X, LATE_Y, LATE_XY)
     back = (BACK_X, BACK_Y, BACK_XY)
@@ -520,16 +533,16 @@
             for number in early:
                 receive(s, number)
         else:
-            for number in early:
-                receive(s, number)
-            solve(s, 1, False)
-            solve(s, 1, True)
             take_images_z(s - 1)
             update_late(s - 1)
             round_late(s)
             for number in z_early + z_late:
                 receive(s, number)
             send(s, *late)
+            for number in early:
+                receive(s, number)
+            solve(s, 1, False)
+            solve(s, 1, True)
         for number in late:
             receive(s, number)
         solve(s, 0, False)
@@ -548,8 +561,7 @@
             solve(s, 1, True)
             send_back(s, (1, 2), back2)
             lax.fori_loop(0, 4, elements, 0)
-            blank_change()
-            blank_total(1)
+            blank_change(0)
         take_back(s, (1, 2), back2)
         clear_total(s)
         images(s, 1)
@@ -562,6 +574,10 @@
         if s < SWEEPS - 1:
             round_early(s + 1)
             send(s + 1, *z_early)
+            blank_total(s + 1)
+            blank_change(s + 1)
+        else:
+            write_early()
         take_images(s, 1)
         take_images(s, 2)
         clear_left()
@@ -570,22 +586,15 @@
             send(s + 1, *z_late)
             send(s + 1, *early)
 
-    for x in range(2):
-        for y in range(2):
-            for z in range(2):
-                block = total[0, x + 1, y + 1, z + 1] + total[1, x + 1, y + 1, z + 1]
-                solution_ref[x, y, 0:63, z, :] = block[16:79]
-                solution_ref[x, y, 63:72, z, :] = block[80:89]
-                lower = total[0, x + 1, y + 1, z, 0:16] + total[1, x + 1, y + 1, z, 0:16]
-                solution_ref[x, y, 72:81, z, :] = lower[0:9]
-                residual_ref[x, y, 0:63, z, :] = left[x, y, z + 1, 16:79]
-                residual_ref[x, y, 63:72, z, :] = left[x, y, z + 1, 80:89]
+    for z in range(2):
+        for k in range(2):
+            residual_ref[0, k, 54:63, z, :] = left[0, k, z + 1, 70:79]
+            residual_ref[k, 0, 63:72, z, :] = left[k, 0, z + 1, 80:89]
     take_images_z(SWEEPS - 1)
     update_late(SWEEPS - 1)
     for x in range(2):
         for y in range(2):
-            for z in range(2):
-                residual_ref[x, y, 72:81, z, :] = left[x, y, z, 0:9]
+            residual_ref[x, y, 72:81, 0, :] = left[x, y, 0, 0:9]
 
     for copy, sends, _ in routes.values():
         if_(sends, copy.wait_send)

time: 71.5 us -> 68.9 us (0.964)
  Pallas kernels: 70.6 us -> 67.8 us
    pallas_call x1, Pallas kernels: 68.6 us -> 65.8 us  [body(): pl.pallas_call(kernel, out_shape=(shape, shape), in_specs=[pl.BlockSpec(m...]
where the time goes in v2:
time: 68.9 us; the launch traced here: 68.6 us
  Pallas kernels  67.8 us (98%)
  between operations  0.8 us (1%)
    pallas_call x1, Pallas kernels, body(): pl.pallas_call(kernel, out_shape=(shape, shape), in_specs=[pl.BlockSpec(m...  65.8 us
    pallas_call x1, Pallas kernels, body(): pl.pallas_call(finish, out_shape=(shape, shape), in_specs=[vmem, vmem], o...  1.93 us

profile of v2, /device:TPU:36, one launch (start us, length us, event | category | flops | bytes accessed | tf_op | source)
XLA Modules:
  0.0 68.6 jit_solution(5584402566288535049)
XLA Ops:
  0.6 65.8 %shard_map.68 = (f32[2,2,81,2,128]{4,3,2,1,0:T(2,128)}, f32[2,2,81,2,128]{4,3,2,1,0:T(2,128)}) custom-call(f32[2,2,81,2,128]{4,3,2,1,0:T(2,128)} %bitcast.8, bf16[2,2,540,2,540]{4,3,2,1,0:T(2,128)(2,1)} %bitcast.6, s32[2,2,2,540]{3,2,1,0:T(2,128)} %order_any.1, f32[2,2,108,2,108]{4,3,2,1,0:T(2,128)} %bitcast.7, s32[2,2,6,2,9]{4,3,2,1,0:T(2,128)} %bitcast.9), custom_call_target="tpu_custom_call" | custom-call | tf_op jit(solution)/shard_map/pallas_call | solution.py:608
  66.5 1.9 %shard_map.69 = (f32[2,2,81,2,128]{4,3,2,1,0:T(2,128)}, f32[2,2,81,2,128]{4,3,2,1,0:T(2,128)}) custom-call(f32[2,2,81,2,128]{4,3,2,1,0:T(2,128)} %get-tuple-element.6.first, f32[2,2,81,2,128]{4,3,2,1,0:T(2,128)} %get-tuple-element.7.second), custom_call_target="tpu_custom_call" | custom-call | tf_op jit(solution)/shard_map/pallas_call | solution.py:661

commit v3 on v2

--- a/solution.py
+++ b/solution.py
@@ -166,9 +166,9 @@
             route(s, xy, out_xy.at[s, layers], in_xy.at[s, layers], (down_x, lower_y, gz), not_first_y, not_last_y)
         for number, rows in (
             (BACK_Z_FIRST, slice(0, 96)),
-            (BACK_Z_Y, slice(96, 192)),
-            (BACK_Z_X, slice(192, 288)),
-            (BACK_Z, slice(288, 448)),
+            (BACK_Z_Y, slice(96, 208)),
+            (BACK_Z_X, slice(208, 320)),
+            (BACK_Z, slice(320, 448)),
         ):
             route(s, number, out_z.at[s, rows], in_z.at[s, rows], (gx, gy, gz - 1), not_first_z, not_last_z)
         for l in (0, 1):
@@ -216,11 +216,11 @@
                 left[x, y, z, 0:9] = start_ref[x, y, 72:81, z, :]
     clear_left()
 
-    def round_early(s):
+    def round_own(s, l):
+        rows = slice(0, 96) if l == 1 else slice(16, 96)
         for x in range(2):
             for y in range(2):
-                rim[s, x + 1, y + 1, 1] = left[x, y, 1].astype(BF16)
-                rim[s, x + 1, y + 1, 2, 16:96] = left[x, y, 2, 16:96].astype(BF16)
+                rim[s, x + 1, y + 1, l, rows] = left[x, y, l, rows].astype(BF16)
 
     def round_late(s):
         for x in range(2):
@@ -228,12 +228,12 @@
                 rim[s, x + 1, y + 1, 0, 0:16] = left[x, y, 0, 0:16].astype(BF16)
 
     def round_faces(s):
-        for l in (1, 2):
-            for k in range(2):
-                rim[s, 1, k + 1, l, 64:80] = left[0, k, l, 64:80].astype(BF16)
-                rim[s, k + 1, 1, l, 80:96] = left[k, 0, l, 80:96].astype(BF16)
-
-    round_early(0)
+        for k in range(2):
+            rim[s, 1, k + 1, 2, 64:80] = left[0, k, 2, 64:80].astype(BF16)
+            rim[s, k + 1, 1, 2, 80:96] = left[k, 0, 2, 80:96].astype(BF16)
+
+    round_own(0, 1)
+    round_own(0, 2)
     round_late(0)
 
     met = 2 + 2 * not_last_y.astype(jnp.int32) + 2 * not_first_y.astype(jnp.int32)
@@ -341,12 +341,17 @@
             for k in (1, 2):
                 out_x[s, l, k - 1, 0:96] = total[s, 0, k, l].astype(BF16)
                 out_x[s, l, k - 1, 96:112] = total[s, 1, k, l, 64:80].astype(BF16)
+        send(s, numbers[0])
+        for l in layers:
+            for k in (1, 2):
                 out_y[s, l, k - 1, 0:96] = total[s, k, 0, l].astype(BF16)
                 out_y[s, l, k - 1, 96:112] = total[s, k, 1, l, 80:96].astype(BF16)
+        send(s, numbers[1])
+        for l in layers:
             out_xy[s, l, 0:96] = total[s, 0, 0, l].astype(BF16)
             out_xy[s, l, 96:112] = total[s, 1, 0, l, 64:80].astype(BF16)
             out_xy[s, l, 112:128] = total[s, 0, 1, l, 80:96].astype(BF16)
-        send(s, *numbers)
+        send(s, numbers[2])
 
     def take_back(s, layers, numbers):
         def from_x():
@@ -370,9 +375,12 @@
         for number, use, then in ((numbers[1], from_y, BACK_Z_Y), (numbers[0], from_x, BACK_Z_X), (numbers[2], from_xy, None)):
             receive(s, number, use)
             if then is not None and layers == (0,):
-                x, y = (1, 2) if then == BACK_Z_Y else (2, 1)
-                m = BLOCK * (2 * x + y - 3)
-                out_z[s, m : m + BLOCK] = total[s, x, y, 0].astype(BF16)
+                if then == BACK_Z_Y:
+                    out_z[s, 96:192] = total[s, 1, 2, 0].astype(BF16)
+                    out_z[s, 192:208] = total[s, 1, 3, 0, 80:96].astype(BF16)
+                else:
+                    out_z[s, 208:304] = total[s, 2, 1, 0].astype(BF16)
+                    out_z[s, 304:320] = total[s, 3, 1, 0, 64:80].astype(BF16)
                 send(s, then)
 
     def send_back_z_first(s):
@@ -380,28 +388,32 @@
         send(s, BACK_Z_FIRST)
 
     def send_back_z(s):
-        out_z[s, 3 * BLOCK : 4 * BLOCK] = total[s, 2, 2, 0].astype(BF16)
-        for k in (1, 2):
-            m = 384 + 16 * (k - 1)
-            out_z[s, m : m + 16] = total[s, 3, k, 0, 64:80].astype(BF16)
-            out_z[s, m + 32 : m + 48] = total[s, k, 3, 0, 80:96].astype(BF16)
+        out_z[s, 320:416] = total[s, 2, 2, 0].astype(BF16)
+        out_z[s, 416:432] = total[s, 3, 2, 0, 64:80].astype(BF16)
+        out_z[s, 432:448] = total[s, 2, 3, 0, 80:96].astype(BF16)
         send(s, BACK_Z)
 
     def take_back_z(s):
-        def use():
-            for x in (1, 2):
-                for y in (1, 2):
-                    m = BLOCK * (2 * x + y - 3)
-                    total[s, x, y, 2] += in_z[s, m : m + BLOCK].astype(F32)
-            for k in (1, 2):
-                m = 384 + 16 * (k - 1)
-                total[s, 3, k, 2, 64:80] += in_z[s, m : m + 16].astype(F32)
-                total[s, k, 3, 2, 80:96] += in_z[s, m + 32 : m + 48].astype(F32)
-
-        receive(s, BACK_Z_FIRST)
-        receive(s, BACK_Z_Y)
-        receive(s, BACK_Z_X)
-        receive(s, BACK_Z, use)
+        def first():
+            total[s, 1, 1, 2] += in_z[s, 0:96].astype(F32)
+
+        def from_y():
+            total[s, 1, 2, 2] += in_z[s, 96:192].astype(F32)
+            total[s, 1, 3, 2, 80:96] += in_z[s, 192:208].astype(F32)
+
+        def from_x():
+            total[s, 2, 1, 2] += in_z[s, 208:304].astype(F32)
+            total[s, 3, 1, 2, 64:80] += in_z[s, 304:320].astype(F32)
+
+        def last():
+            total[s, 2, 2, 2] += in_z[s, 320:416].astype(F32)
+            total[s, 3, 2, 2, 64:80] += in_z[s, 416:432].astype(F32)
+            total[s, 2, 3, 2, 80:96] += in_z[s, 432:448].astype(F32)
+
+        receive(s, BACK_Z_FIRST, first)
+        receive(s, BACK_Z_Y, from_y)
+        receive(s, BACK_Z_X, from_x)
+        receive(s, BACK_Z, last)
 
     def clear_total(s):
         @pl.when(first_y)
@@ -436,17 +448,18 @@
                 change[s, x, y + 1, l, 80:96] += image[128:144]
 
     def send_images(s, l):
-        if l == 2:
-            for x in (1, 2):
-                for y in (1, 2):
-                    m = 16 * (2 * x + y - 3)
-                    out_iz[s, m : m + 16] = change[s, x, y, 2, 0:16].astype(BF16)
-            send(s, IMAGE_Z)
         for k in (1, 2):
             m = 16 * (k - 1)
             out_ix[s, l - 1, m : m + 16] = change[s, 3, k, l, 64:80].astype(BF16)
             out_iy[s, l - 1, m : m + 16] = change[s, k, 3, l, 80:96].astype(BF16)
         send(s, IMAGE_X + l - 1, IMAGE_Y + l - 1)
+
+    def send_images_z(s):
+        for x in (1, 2):
+            for y in (1, 2):
+                m = 16 * (2 * x + y - 3)
+                out_iz[s, m : m + 16] = change[s, x, y, 2, 0:16].astype(BF16)
+        send(s, IMAGE_Z)
 
     def take_images(s, l):
         def from_x():
@@ -469,11 +482,11 @@
 
         receive(s, IMAGE_Z, use)
 
-    def update_early(s):
+    def update_own(s, l):
+        rows = slice(0, 96) if l == 1 else slice(16, 96)
         for x in (1, 2):
             for y in (1, 2):
-                left[x - 1, y - 1, 1] -= change[s, x, y, 1]
-                left[x - 1, y - 1, 2, 16:96] -= change[s, x, y, 2, 16:96]
+                left[x - 1, y - 1, l, rows] -= change[s, x, y, l, rows]
         clear_left()
 
     def update_late(s):
@@ -563,28 +576,40 @@
             lax.fori_loop(0, 4, elements, 0)
             blank_change(0)
         take_back(s, (1, 2), back2)
-        clear_total(s)
-        images(s, 1)
-        send_images(s, 1)
-        take_back_z(s)
-        clear_total(s)
-        images(s, 2)
-        send_images(s, 2)
-        update_early(s)
         if s < SWEEPS - 1:
-            round_early(s + 1)
+            take_back_z(s)
+            clear_total(s)
+            images(s, 2)
+            send_images(s, 2)
+            update_own(s, 2)
+            round_own(s + 1, 2)
             send(s + 1, *z_early)
+            send_images_z(s)
+            images(s, 1)
+            send_images(s, 1)
+            update_own(s, 1)
+            take_images(s, 2)
+            round_faces(s + 1)
+            send(s + 1, *z_late)
             blank_total(s + 1)
+            take_images(s, 1)
+            round_own(s + 1, 1)
+            send(s + 1, *early)
             blank_change(s + 1)
         else:
+            clear_total(s)
+            images(s, 1)
+            send_images(s, 1)
+            take_back_z(s)
+            clear_total(s)
+            images(s, 2)
+            send_images_z(s)
+            send_images(s, 2)
+            update_own(s, 1)
+            update_own(s, 2)
             write_early()
-        take_images(s, 1)
-        take_images(s, 2)
-        clear_left()
-        if s < SWEEPS - 1:
-            round_faces(s + 1)
-            send(s + 1, *z_late)
-            send(s + 1, *early)
+            take_images(s, 1)
+            take_images(s, 2)
 
     for z in range(2):
         for k in range(2):

time: 68.9 us -> 68.5 us (level)
  Pallas kernels: 67.8 us -> 67 us
    pallas_call x1, Pallas kernels: 65.8 us -> 65.1 us  [body(): pl.pallas_call(kernel, out_shape=(shape, shape), in_specs=[pl.BlockSpec(m...]
where the time goes in v3:
time: 68.5 us; the launch traced here: 67.8 us
  Pallas kernels  67 us (98%)
  between operations  0.8 us (1%)
    pallas_call x1, Pallas kernels, body(): pl.pallas_call(kernel, out_shape=(shape, shape), in_specs=[pl.BlockSpec(m...  65.1 us
    pallas_call x1, Pallas kernels, body(): pl.pallas_call(finish, out_shape=(shape, shape), in_specs=[vmem, vmem], o...  1.93 us

profile of v3, /device:TPU:36, one launch (start us, length us, event | category | flops | bytes accessed | tf_op | source)
XLA Modules:
  0.0 67.8 jit_solution(17247089452007045064)
XLA Ops:
  0.6 65.1 %shard_map.68 = (f32[2,2,81,2,128]{4,3,2,1,0:T(2,128)}, f32[2,2,81,2,128]{4,3,2,1,0:T(2,128)}) custom-call(f32[2,2,81,2,128]{4,3,2,1,0:T(2,128)} %bitcast.8, bf16[2,2,540,2,540]{4,3,2,1,0:T(2,128)(2,1)} %bitcast.6, s32[2,2,2,540]{3,2,1,0:T(2,128)} %order_any.1, f32[2,2,108,2,108]{4,3,2,1,0:T(2,128)} %bitcast.7, s32[2,2,6,2,9]{4,3,2,1,0:T(2,128)} %bitcast.9), custom_call_target="tpu_custom_call" | custom-call | tf_op jit(solution)/shard_map/pallas_call | solution.py:633
  65.8 1.9 %shard_map.69 = (f32[2,2,81,2,128]{4,3,2,1,0:T(2,128)}, f32[2,2,81,2,128]{4,3,2,1,0:T(2,128)}) custom-call(f32[2,2,81,2,128]{4,3,2,1,0:T(2,128)} %get-tuple-element.6.first, f32[2,2,81,2,128]{4,3,2,1,0:T(2,128)} %get-tuple-element.7.second), custom_call_target="tpu_custom_call" | custom-call | tf_op jit(solution)/shard_map/pallas_call | solution.py:686

commit v4 on v3

--- a/solution.py
+++ b/solution.py
@@ -298,7 +298,7 @@
             stars[c, i] = lax.dot_general(rows, pick, dims_nt, preferred_element_type=F32).astype(BF16)
             return carry
 
-        lax.fori_loop(first, last, vertex, 0)
+        lax.fori_loop(first, last, vertex, 0, unroll=True)
 
     def star(s, c, x, y):
         pieces = []

time: 68.5 us -> 68.2 us (level)
  no operation moved by 1% of the time
where the time goes in v4:
time: 68.2 us; the launch traced here: 67.9 us
  Pallas kernels  67.1 us (98%)
  between operations  0.8 us (1%)
    pallas_call x1, Pallas kernels, body(): pl.pallas_call(kernel, out_shape=(shape, shape), in_specs=[pl.BlockSpec(m...  65.2 us
    pallas_call x1, Pallas kernels, body(): pl.pallas_call(finish, out_shape=(shape, shape), in_specs=[vmem, vmem], o...  1.93 us

profile of v4, /device:TPU:36, one launch (start us, length us, event | category | flops | bytes accessed | tf_op | source)
XLA Modules:
  0.0 67.9 jit_solution(2531304905673060531)
XLA Ops:
  0.6 65.2 %shard_map.68 = (f32[2,2,81,2,128]{4,3,2,1,0:T(2,128)}, f32[2,2,81,2,128]{4,3,2,1,0:T(2,128)}) custom-call(f32[2,2,81,2,128]{4,3,2,1,0:T(2,128)} %bitcast.8, bf16[2,2,540,2,540]{4,3,2,1,0:T(2,128)(2,1)} %bitcast.6, s32[2,2,2,540]{3,2,1,0:T(2,128)} %order_any.1, f32[2,2,108,2,108]{4,3,2,1,0:T(2,128)} %bitcast.7, s32[2,2,6,2,9]{4,3,2,1,0:T(2,128)} %bitcast.9), custom_call_target="tpu_custom_call" | custom-call | tf_op jit(solution)/shard_map/pallas_call | solution.py:633
  65.8 1.9 %shard_map.69 = (f32[2,2,81,2,128]{4,3,2,1,0:T(2,128)}, f32[2,2,81,2,128]{4,3,2,1,0:T(2,128)}) custom-call(f32[2,2,81,2,128]{4,3,2,1,0:T(2,128)} %get-tuple-element.6.first, f32[2,2,81,2,128]{4,3,2,1,0:T(2,128)} %get-tuple-element.7.second), custom_call_target="tpu_custom_call" | custom-call | tf_op jit(solution)/shard_map/pallas_call | solution.py:686
